TPU v7x, 32 devices: a whole 2x2x4 slice. The times are simulated.
32 devices in a mesh: vox: 4 (over y, core), fas: 8 (over z, x).
Axes of the slice: x: 2, y: 2, z: 4, core: 2. Of those that a mesh axis runs over, the one named last changes fastest.
Arguments:
- signal: float32 [64, 6144], P('vox', 'fas'), may hold values from -6 to 6
- initial_weights: float32 [262144], P('fas'), may hold values from 0.1 to 2
- coefficients: bfloat16 [8192, 4096], P(('vox', 'fas')), may hold values from 0 to 0.032958984
- block_rows: int32 [8192], P(('vox', 'fas')), may hold values from 0 to 63, as said below
- block_cols: int32 [8192], P(('vox', 'fas')), may hold values from 0 to 4095, as said below
- block_atoms: int32 [8192, 64], P(('vox', 'fas')), may hold values from 0 to 359
- block_count: int32 [32], P(('vox', 'fas')), may hold values from 64 to 256, as said below
- dictionary: bfloat16 [360, 96], replicated, may hold values from -6 to 6
Outputs:
- weights: float32 [262144], P('fas')
- residual: float32 [64, 6144], P('vox', 'fas')
Inputs may be any that keep to these rules, and one draw needn't show every extreme that they name: Block slots are stored device by device: the device with vox index i and fas index f holds slots (i * 8 + f) * 256 to (i * 8 + f + 1) * 256 - 1, and every block_rows value there lies in i * 16 to (i + 1) * 16 - 1. For the slots of the device with fas index f, every block_cols value lies in f * 512 to (f + 1) * 512 - 1. `block_count`: entry i * 8 + f is the number of live slots of the device with vox index i and fas index f, its first slots; some device has all 256 live.
All inputs are finite; a program needn't handle non-finite values.
Results may differ from a plain program's by a relative error of at most 0.0003.
Values sent between devices are 32-bit elements; how exact they have to be, the bound alone decides.
No kernel may reach another device: no remote copies, remote signals or barrier semaphores. Data moves between devices by JAX's collectives and lax.ppermute only.
A program may use at most 128 MiB of HBM per device.

v0:
```python
import functools

import jax
import jax.numpy as jnp
from jax import lax
from jax.experimental import pallas as pl
from jax.experimental.pallas import tpu as pltpu
from jax.sharding import PartitionSpec as P

BV = 64
BF = 64
DIRS = 96
ITERS = 5
LANES = 128
GROUP = 4
BUILD = 8
UNROLL = 40
PACK = BV * DIRS // LANES
HALF = BV // 2
QUART = BV // 4
VMEM_LIMIT = 16 * 1024 * 1024


def group_cap(slots, rows):
    groups = slots // GROUP + rows
    return -(-groups // UNROLL) * UNROLL


def lane_ids(rows):
    return lax.broadcasted_iota(jnp.int32, (rows, LANES), 1)


def setup_kernel(slot_ref, turns_ref, coef_ref, atom_ref, dict_ref, cp_ref, at_ref, a_ref):
    atoms_pad = dict_ref.shape[1]
    left32 = lane_ids(HALF) < BF
    left1 = lane_ids(1) < BF
    atom_ids = lax.broadcasted_iota(jnp.int32, (atoms_pad, LANES), 0)

    def build(q):
        tops, bottoms, marks = [], [], []
        for pair in range(GROUP // 2):
            s0 = slot_ref[q * GROUP + 2 * pair]
            s1 = slot_ref[q * GROUP + 2 * pair + 1]
            k0 = jnp.maximum(s0, 0)
            k1 = jnp.maximum(s1, 0)
            m0 = (s0 >= 0).astype(jnp.float32)
            m1 = (s1 >= 0).astype(jnp.float32)
            c0 = coef_ref[k0].astype(jnp.float32) * m0
            c1 = coef_ref[k1].astype(jnp.float32) * m1
            tops.append(jnp.where(left32, c0, pltpu.roll(c1, BF, 1)))
            bottoms.append(jnp.where(left32, pltpu.roll(c0, BF, 1), c1))
            ids = jnp.where(left1, atom_ref[pl.ds(k0, 1), :], atom_ref[pl.ds(k1, 1), :])
            marks.append((atom_ids == ids).astype(jnp.float32).astype(jnp.bfloat16))
        top = jnp.concatenate(tops, axis=1)
        bottom = jnp.concatenate(bottoms, axis=1)
        cp_ref[q] = jnp.concatenate([top, bottom], axis=0).astype(jnp.bfloat16)
        marked = jnp.concatenate(marks, axis=1)
        table = jnp.dot(dict_ref[...], marked, preferred_element_type=jnp.float32)
        at_ref[q] = table.astype(jnp.bfloat16)
        a_ref[q] = table.T.astype(jnp.bfloat16)

    def turn(t, carry):
        for n in range(BUILD):
            build(t * BUILD + n)
        return carry

    lax.fori_loop(0, turns_ref[0] * (UNROLL // BUILD), turn, 0)


def sort_slots(rows, cols, count, vox_rows, cap):
    i32 = jnp.int32
    slots = rows.shape[0]
    k = jnp.arange(slots, dtype=i32)
    rows = jnp.where(k < count, rows, vox_rows)
    r = jnp.arange(vox_rows, dtype=i32)
    member = rows[:, None] == r[None, :]
    groups = (jnp.sum(member.astype(i32), axis=0) + GROUP - 1) // GROUP
    start = jnp.sum(jnp.where(r[:, None] < r[None, :], groups[:, None], 0), axis=0)
    total = jnp.sum(groups)
    before = (rows[:, None] == rows[None, :]) & (k[None, :] < k[:, None])
    rank = jnp.sum(before.astype(i32), axis=1)
    first = jnp.sum(jnp.where(member, start[None, :], 0), axis=1)
    place = jnp.where(rows < vox_rows, first * GROUP + rank, -1)
    chosen = jnp.arange(cap * GROUP, dtype=i32)[:, None] == place[None, :]
    slot = jnp.sum(jnp.where(chosen, k[None, :] + 1, 0), axis=1) - 1
    col = jnp.sum(jnp.where(chosen, cols[None, :], 0), axis=1)
    q = jnp.arange(cap, dtype=i32)
    row = jnp.sum((start[None, :] <= q[:, None]).astype(i32), axis=1) - 1
    turns = (total + UNROLL - 1) // UNROLL
    return slot, jnp.concatenate([col, row, turns[None]]), turns[None]


def spread_table(values, table_ref):
    rows = values.shape[0]
    left = lane_ids(rows) < BF
    turned = pltpu.roll(values, BF, 1)
    table_ref[pl.ds(0, rows, stride=2), :] = jnp.where(left, values, turned)
    table_ref[pl.ds(1, rows, stride=2), :] = jnp.where(left, turned, values)


def run_forward(cap, meta_ref, cp_ref, a_ref, table_ref, acc_ref):
    left = lane_ids(1) < BF

    def turn(t, carry):
        outs = []
        for n in range(UNROLL):
            q = t * UNROLL + n
            u = []
            for pair in range(GROUP // 2):
                p = q * GROUP + 2 * pair
                u0 = table_ref[pl.ds(meta_ref[p], 1), :]
                u1 = table_ref[pl.ds(meta_ref[p + 1], 1), :]
                u.append(jnp.where(left, u0, u1))
            scaled = cp_ref[q].astype(jnp.float32) * jnp.concatenate(u, axis=1)
            high = scaled.astype(jnp.bfloat16)
            low = (scaled - high.astype(jnp.float32)).astype(jnp.bfloat16)
            both = jnp.concatenate([high, low], axis=0)
            out = jnp.dot(both, a_ref[q], preferred_element_type=jnp.float32)
            outs.append(out[:BV] + out[BV:])
        for n in range(UNROLL):
            r = meta_ref[cap * GROUP + t * UNROLL + n]
            acc_ref[r] = acc_ref[r] + outs[n]
        return carry

    lax.fori_loop(0, meta_ref[cap * (GROUP + 1)], turn, 0)


def pack_rows(acc_ref, out_ref):
    lane = lane_ids(QUART)
    for r in range(acc_ref.shape[0]):
        last = acc_ref[r, 3 * QUART :, :]
        for i in range(3):
            tail = pltpu.roll(last, DIRS - 32 * i, 1)
            out_ref[pl.ds(r * PACK + i * QUART, QUART), :] = jnp.where(
                lane < DIRS, acc_ref[r, i * QUART : (i + 1) * QUART, :], tail
            )


def first_kernel(cap, meta_ref, w_ref, sig_ref, cp_ref, a_ref, out_ref, table_ref, acc_ref):
    spread_table(w_ref[...], table_ref)
    acc_ref[...] = sig_ref[...]
    run_forward(cap, meta_ref, cp_ref, a_ref, table_ref, acc_ref)
    pack_rows(acc_ref, out_ref)


def image_kernel(cap, meta_ref, g_ref, w_ref, cp_ref, a_ref, out_ref, p_ref, sq_ref, table_ref, acc_ref):
    gradient = g_ref[...]
    projected = jnp.where((w_ref[...] > 0) | (gradient < 0), gradient, 0.0)
    p_ref[...] = projected
    sq_ref[...] = jnp.sum((projected * projected).reshape(-1, 8, LANES), axis=0)
    spread_table(projected, table_ref)
    acc_ref[...] = jnp.zeros_like(acc_ref)
    run_forward(cap, meta_ref, cp_ref, a_ref, table_ref, acc_ref)
    pack_rows(acc_ref, out_ref)


def update_kernel(
    cap,
    vox_total,
    last,
    meta_ref,
    sums_ref,
    p_ref,
    w_ref,
    sig_ref,
    cp_ref,
    a_ref,
    out_ref,
    new_ref,
    table_ref,
    acc_ref,
):
    sums = jnp.sum(sums_ref[...], axis=0)
    upper = lax.broadcasted_iota(jnp.int32, (8, LANES), 0) < 4
    image_sq = jnp.sum(jnp.where(upper, sums, 0.0), keepdims=True)
    grad_sq = jnp.sum(jnp.where(upper, 0.0, sums), keepdims=True) * (1.0 / vox_total)
    step = grad_sq / (image_sq + 1e-6)
    updated = jnp.maximum(w_ref[...] - step * p_ref[...], 0.0)
    new_ref[...] = updated
    spread_table(updated, table_ref)
    acc_ref[...] = sig_ref[...]
    run_forward(cap, meta_ref, cp_ref, a_ref, table_ref, acc_ref)
    if last:
        out_ref[...] = acc_ref[...]
    else:
        pack_rows(acc_ref, out_ref)


def backward_kernel(cap, vox_rows, meta_ref, res_ref, cp_ref, at_ref, out_ref, split_ref, table_ref):
    lane = lane_ids(QUART)
    for r in range(vox_rows):
        packed = [res_ref[pl.ds(r * PACK + i * QUART, QUART), :] for i in range(3)]
        turned = [pltpu.roll(packed[i], 32 * (i + 1), 1) for i in range(3)]
        last = jnp.where(lane < 32, turned[0], jnp.where(lane < 64, turned[1], turned[2]))
        whole = jnp.concatenate(packed + [last], axis=0)
        whole = jnp.where(lane_ids(BV) < DIRS, whole, 0.0)
        high = whole.astype(jnp.bfloat16)
        low = (whole - high.astype(jnp.float32)).astype(jnp.bfloat16)
        split_ref[r] = jnp.concatenate([high, low], axis=0)
    table_ref[...] = jnp.zeros_like(table_ref)
    left = lane_ids(1) < BF

    def turn(t, carry):
        sums = []
        for n in range(UNROLL):
            q = t * UNROLL + n
            r = meta_ref[cap * GROUP + q]
            part = jnp.dot(split_ref[r], at_ref[q], preferred_element_type=jnp.float32)
            part = (part[:BV] + part[BV:]) * cp_ref[q].astype(jnp.float32)
            sums.append(jnp.sum(part, axis=0, keepdims=True))
        for n in range(UNROLL):
            for pair in range(GROUP // 2):
                p = (t * UNROLL + n) * GROUP + 2 * pair
                row = sums[n][:, pair * LANES : (pair + 1) * LANES]
                c0 = pl.ds(meta_ref[p], 1)
                table_ref[c0, :] = table_ref[c0, :] + jnp.where(left, row, 0.0)
                c1 = pl.ds(meta_ref[p + 1], 1)
                table_ref[c1, :] = table_ref[c1, :] + jnp.where(left, 0.0, row)
        return carry

    lax.fori_loop(0, meta_ref[cap * (GROUP + 1)], turn, 0)
    rows = out_ref.shape[0]
    even = table_ref[pl.ds(0, rows, stride=2), :]
    odd = table_ref[pl.ds(1, rows, stride=2), :]
    even = even + pltpu.roll(even, BF, 1)
    odd = odd + pltpu.roll(odd, BF, 1)
    out_ref[...] = jnp.where(lane_ids(rows) < BF, even, odd)


def share_kernel(shares_ref, out_ref):
    total = jnp.sum(shares_ref[...], axis=0)
    for i in range(out_ref.shape[0]):
        out_ref[i] = total


def norm_kernel(shares_ref, sq_ref, out_ref):
    image = jnp.sum(shares_ref[...], axis=0)
    image_sq = jnp.sum((image * image).reshape(-1, 8, LANES), axis=0)
    sums = jnp.concatenate([image_sq[:4] + image_sq[4:], sq_ref[:4] + sq_ref[4:]], axis=0)

    def copy_out(i, carry):
        out_ref[i] = sums
        return carry

    lax.fori_loop(0, out_ref.shape[0], copy_out, 0)


def call(kernel, outs, ins, scratch=()):
    spaces = {"v": pltpu.VMEM, "s": pltpu.SMEM}
    run = pl.pallas_call(
        kernel,
        out_shape=tuple(
            pltpu.VMEM(shape, dtype) if kind == "v" else jax.ShapeDtypeStruct(shape, dtype)
            for shape, dtype, kind in outs
        ),
        in_specs=[pl.BlockSpec(memory_space=spaces[kind]) for kind in ins],
        out_specs=tuple(pl.BlockSpec(memory_space=spaces[kind]) for _, _, kind in outs),
        scratch_shapes=list(scratch),
        compiler_params=pltpu.CompilerParams(vmem_limit_bytes=VMEM_LIMIT),
    )

    def placed(*args):
        return run(
            *(
                pltpu.with_memory_space_constraint(x, pltpu.VMEM) if kind == "v" else x
                for x, kind in zip(args, ins)
            )
        )

    return placed


def local(
    n_vox,
    n_fas,
    signal,
    initial_weights,
    coefficients,
    block_rows,
    block_cols,
    block_atoms,
    block_count,
    dictionary,
):
    f32, bf16, i32 = jnp.float32, jnp.bfloat16, jnp.int32
    vox_rows = signal.shape[0]
    fas_rows = initial_weights.shape[0] // BF
    slots = coefficients.shape[0]
    cap = group_cap(slots, vox_rows)
    atoms = dictionary.shape[0]
    atoms_pad = -(-atoms // LANES) * LANES
    wide = GROUP * BF
    half_rows = fas_rows // 2

    coef_view = coefficients.reshape(slots, HALF, LANES)
    atom_view = jnp.concatenate([block_atoms, block_atoms], axis=1)
    dict_t = jnp.pad(dictionary.T, ((0, LANES - DIRS), (0, atoms_pad - atoms)))
    fas_place = lax.axis_index("fas")
    slot, meta, turns = sort_slots(
        block_rows - lax.axis_index("vox") * vox_rows,
        block_cols - fas_place * fas_rows,
        block_count[0],
        vox_rows,
        cap,
    )
    cp, at, a = call(
        setup_kernel,
        [
            ((cap, BV, wide), bf16, "v"),
            ((cap, LANES, wide), bf16, "v"),
            ((cap, wide, LANES), bf16, "v"),
        ],
        "ssvvv",
    )(slot, turns, coef_view, atom_view, dict_t)

    own = signal.shape[1] // DIRS // 2
    negative = -signal.reshape(vox_rows, own, 2, DIRS).transpose(0, 2, 1, 3)
    negative = jnp.pad(negative, ((0, 0), (0, 0), (0, 0), (0, LANES - DIRS)))
    sig = lax.dynamic_update_slice(
        jnp.zeros((vox_rows, 2, HALF, LANES), f32), negative, (0, 0, fas_place * own, 0)
    ).reshape(vox_rows, BV, LANES)

    image_rows = vox_rows * PACK
    table = pltpu.VMEM((fas_rows, LANES), f32)
    acc = pltpu.VMEM((vox_rows, BV, LANES), f32)
    image_out = ((image_rows, LANES), f32, "v")
    flat_out = ((half_rows, LANES), f32, "v")

    def swap(x, axis):
        return lax.all_to_all(x, axis, 0, 0)

    share_rows = image_rows // n_fas

    def collect(partial):
        return swap(partial.reshape(n_fas, share_rows, LANES), "fas")

    weights = initial_weights.reshape(half_rows, LANES)
    (partial,) = call(
        functools.partial(first_kernel, cap), [image_out], "svvvv", [table, acc]
    )(meta, weights, sig, cp, a)
    for sweep in range(ITERS):
        last = sweep == ITERS - 1
        (residual,) = call(share_kernel, [((n_fas, share_rows, LANES), f32, "v")], "v")(
            collect(partial)
        )
        whole = swap(residual, "fas")
        (gradient,) = call(
            functools.partial(backward_kernel, cap, vox_rows),
            [flat_out],
            "svvv",
            [pltpu.VMEM((vox_rows, 2 * BV, LANES), bf16), table],
        )(meta, whole.reshape(image_rows, LANES), cp, at)
        bit = 1
        while bit < n_vox:
            gradient = gradient + lax.ppermute(
                gradient, "vox", [(i, i ^ bit) for i in range(n_vox)]
            )
            bit *= 2
        partial, projected, proj_sq = call(
            functools.partial(image_kernel, cap),
            [image_out, flat_out, ((8, LANES), f32, "v")],
            "svvvv",
            [table, acc],
        )(meta, gradient, weights, cp, a)
        (sums,) = call(norm_kernel, [((n_vox * n_fas, 8, LANES), f32, "v")], "vv")(
            collect(partial), proj_sq
        )
        sums = swap(sums, ("vox", "fas"))
        out = ((vox_rows, BV, LANES), f32, "v") if last else image_out
        partial, weights = call(
            functools.partial(update_kernel, cap, n_vox, last),
            [out, flat_out],
            "svvvvvv",
            [table, acc],
        )(meta, sums, projected, weights, sig, cp, a)
    final = partial.reshape(vox_rows, 2, n_fas, own, LANES)[..., :DIRS].transpose(2, 0, 3, 1, 4)
    final = swap(final.reshape(n_fas, vox_rows, own * 2 * DIRS), "fas")
    return (weights.reshape(-1), jnp.sum(final, axis=0))


def solution(mesh):
    placed = (
        P("vox", "fas"),
        P("fas"),
        P(("vox", "fas"), None),
        P(("vox", "fas")),
        P(("vox", "fas")),
        P(("vox", "fas"), None),
        P(("vox", "fas")),
        P(),
    )
    return jax.shard_map(
        functools.partial(local, mesh.shape["vox"], mesh.shape["fas"]),
        mesh=mesh,
        in_specs=placed,
        out_specs=(P("fas"), P("vox", "fas")),
        check_vma=False,
    )
```

profile of v0, /device:TPU:0, one launch (start us, length us, event | category | flops | bytes accessed | tf_op | source)
XLA Modules:
  0.0 395.1 jit_solution(11188622558673201265)
XLA Ops:
  5.5 2.1 copy.22
  8.2 4.0 %shard_map.95 = (bf16[80,64,256]{2,1,0:T(8,128)(2,1)S(1)}, bf16[80,128,256]{2,1,0:T(8,128)(2,1)S(1)}, bf16[80,256,128]{2,1,0:T(8,128)(2,1)S(1)}) custom-call(s32[320]{0:T(512)S(1)} %broadcast_add_fusion.slot_ref, s32[1]{0:T(128)} %bitcast.1.turns_ref, bf16[256,32,128]{2,1,0:T(8,128)(2,1)S(1)} %bitcast.40, s32[256,128]{1,0:T(8,128)S(1)} %pad_add_fusion.atom_ref, ...), custom_call_target="tpu_custom_call" | custom-call | tf_op jit(solution)/shard_map/pallas_call | solution.py:263
  12.3 1.7 shard_map.96
  14.0 23.3 %all_to_all.105.shares_ref = f32[8,96,128]{2,1,0:T(8,128)S(1)} all-to-all(f32[8,96,128]{2,1,0:T(8,128)S(1)} %bitcast.46), channel_id=1, replica_groups=mesh['vox'=4,'fas'=8] {'fas'}, dimensions={0} | all-to-all | bytes 786432 | tf_op jit(solution)/shard_map/all_to_all | solution.py:330
  37.4 15.5 %all_to_all.106 = f32[8,96,128]{2,1,0:T(8,128)S(1)} all-to-all(f32[8,96,128]{2,1,0:T(8,128)S(1)} %shard_map.97), channel_id=1, replica_groups=mesh['vox'=4,'fas'=8] {'fas'}, dimensions={0} | all-to-all | bytes 786432 | tf_op jit(solution)/shard_map/all_to_all | solution.py:330
  52.8 2.1 shard_map.98
  55.0 1.3 collective-permute-done
  56.4 1.5 collective-permute-start.1
  57.9 4.1 %collective-permute-done.1 = f32[256,128]{1,0:T(8,128)S(1)} collective-permute-done((f32[256,128]{1,0:T(8,128)S(1)}, f32[256,128]{1,0:T(8,128)S(1)}, u32[]{:S(2)}, u32[]{:S(2)}) %collective-permute-start.1) | collective-permute-done | bytes 131104 | tf_op jit(solution)/shard_map/ppermute | solution.py:355
  62.0 1.7 shard_map.99
  63.7 16.4 %all_to_all.107.shares_ref = f32[8,96,128]{2,1,0:T(8,128)S(1)} all-to-all(f32[8,96,128]{2,1,0:T(8,128)S(1)} %bitcast.54), channel_id=1, replica_groups=mesh['vox'=4,'fas'=8] {'fas'}, dimensions={0} | all-to-all | bytes 786432 | tf_op jit(solution)/shard_map/all_to_all | solution.py:330
  80.4 10.7 %all_to_all.108.sums_ref = f32[32,8,128]{2,1,0:T(8,128)S(1)} all-to-all(f32[32,8,128]{2,1,0:T(8,128)S(1)} %shard_map.100), channel_id=1, replica_groups=mesh['vox'=4,'fas'=8] {'vox','fas'}, dimensions={0} | all-to-all | bytes 262144 | tf_op jit(solution)/shard_map/all_to_all | solution.py:330
  91.0 1.9 shard_map.101
  92.9 16.2 %all_to_all.109.shares_ref = f32[8,96,128]{2,1,0:T(8,128)S(1)} all-to-all(f32[8,96,128]{2,1,0:T(8,128)S(1)} %bitcast.55), channel_id=1, replica_groups=mesh['vox'=4,'fas'=8] {'fas'}, dimensions={0} | all-to-all | bytes 786432 | tf_op jit(solution)/shard_map/all_to_all | solution.py:330
  109.1 15.3 %all_to_all.110 = f32[8,96,128]{2,1,0:T(8,128)S(1)} all-to-all(f32[8,96,128]{2,1,0:T(8,128)S(1)} %shard_map.102), channel_id=1, replica_groups=mesh['vox'=4,'fas'=8] {'fas'}, dimensions={0} | all-to-all | bytes 786432 | tf_op jit(solution)/shard_map/all_to_all | solution.py:330
  124.5 2.1 shard_map.103
  128.6 5.0 %collective-permute-done.3 = f32[256,128]{1,0:T(8,128)S(1)} collective-permute-done((f32[256,128]{1,0:T(8,128)S(1)}, f32[256,128]{1,0:T(8,128)S(1)}, u32[]{:S(2)}, u32[]{:S(2)}) %collective-permute-start.3) | collective-permute-done | bytes 131104 | tf_op jit(solution)/shard_map/ppermute | solution.py:355
  133.6 1.7 shard_map.104
  135.3 16.4 %all_to_all.111.shares_ref = f32[8,96,128]{2,1,0:T(8,128)S(1)} all-to-all(f32[8,96,128]{2,1,0:T(8,128)S(1)} %bitcast.56), channel_id=1, replica_groups=mesh['vox'=4,'fas'=8] {'fas'}, dimensions={0} | all-to-all | bytes 786432 | tf_op jit(solution)/shard_map/all_to_all | solution.py:330
  152.0 9.9 %all_to_all.112.sums_ref = f32[32,8,128]{2,1,0:T(8,128)S(1)} all-to-all(f32[32,8,128]{2,1,0:T(8,128)S(1)} %shard_map.105), channel_id=1, replica_groups=mesh['vox'=4,'fas'=8] {'vox','fas'}, dimensions={0} | all-to-all | bytes 262144 | tf_op jit(solution)/shard_map/all_to_all | solution.py:330
  161.8 1.9 shard_map.106
  163.7 16.2 %all_to_all.113.shares_ref = f32[8,96,128]{2,1,0:T(8,128)S(1)} all-to-all(f32[8,96,128]{2,1,0:T(8,128)S(1)} %bitcast.51), channel_id=1, replica_groups=mesh['vox'=4,'fas'=8] {'fas'}, dimensions={0} | all-to-all | bytes 786432 | tf_op jit(solution)/shard_map/all_to_all | solution.py:330
  179.9 15.3 %all_to_all.114 = f32[8,96,128]{2,1,0:T(8,128)S(1)} all-to-all(f32[8,96,128]{2,1,0:T(8,128)S(1)} %shard_map.107), channel_id=1, replica_groups=mesh['vox'=4,'fas'=8] {'fas'}, dimensions={0} | all-to-all | bytes 786432 | tf_op jit(solution)/shard_map/all_to_all | solution.py:330
  195.3 2.3 shard_map.108
  199.6 5.0 %collective-permute-done.5 = f32[256,128]{1,0:T(8,128)S(1)} collective-permute-done((f32[256,128]{1,0:T(8,128)S(1)}, f32[256,128]{1,0:T(8,128)S(1)}, u32[]{:S(2)}, u32[]{:S(2)}) %collective-permute-start.5) | collective-permute-done | bytes 131104 | tf_op jit(solution)/shard_map/ppermute | solution.py:355
  204.6 1.7 shard_map.109
  206.3 16.4 %all_to_all.115.shares_ref = f32[8,96,128]{2,1,0:T(8,128)S(1)} all-to-all(f32[8,96,128]{2,1,0:T(8,128)S(1)} %bitcast.57), channel_id=1, replica_groups=mesh['vox'=4,'fas'=8] {'fas'}, dimensions={0} | all-to-all | bytes 786432 | tf_op jit(solution)/shard_map/all_to_all | solution.py:330
  222.9 9.9 %all_to_all.116.sums_ref = f32[32,8,128]{2,1,0:T(8,128)S(1)} all-to-all(f32[32,8,128]{2,1,0:T(8,128)S(1)} %shard_map.110), channel_id=1, replica_groups=mesh['vox'=4,'fas'=8] {'vox','fas'}, dimensions={0} | all-to-all | bytes 262144 | tf_op jit(solution)/shard_map/all_to_all | solution.py:330
  232.8 1.9 shard_map.111
  234.7 16.2 %all_to_all.117.shares_ref = f32[8,96,128]{2,1,0:T(8,128)S(1)} all-to-all(f32[8,96,128]{2,1,0:T(8,128)S(1)} %bitcast.52), channel_id=1, replica_groups=mesh['vox'=4,'fas'=8] {'fas'}, dimensions={0} | all-to-all | bytes 786432 | tf_op jit(solution)/shard_map/all_to_all | solution.py:330
  250.9 15.3 %all_to_all.118 = f32[8,96,128]{2,1,0:T(8,128)S(1)} all-to-all(f32[8,96,128]{2,1,0:T(8,128)S(1)} %shard_map.112), channel_id=1, replica_groups=mesh['vox'=4,'fas'=8] {'fas'}, dimensions={0} | all-to-all | bytes 786432 | tf_op jit(solution)/shard_map/all_to_all | solution.py:330
  266.2 2.1 shard_map.113
  270.4 5.0 %collective-permute-done.7 = f32[256,128]{1,0:T(8,128)S(1)} collective-permute-done((f32[256,128]{1,0:T(8,128)S(1)}, f32[256,128]{1,0:T(8,128)S(1)}, u32[]{:S(2)}, u32[]{:S(2)}) %collective-permute-start.7) | collective-permute-done | bytes 131104 | tf_op jit(solution)/shard_map/ppermute | solution.py:355
  275.4 1.7 shard_map.114
  277.1 16.4 %all_to_all.119.shares_ref = f32[8,96,128]{2,1,0:T(8,128)S(1)} all-to-all(f32[8,96,128]{2,1,0:T(8,128)S(1)} %bitcast.58), channel_id=1, replica_groups=mesh['vox'=4,'fas'=8] {'fas'}, dimensions={0} | all-to-all | bytes 786432 | tf_op jit(solution)/shard_map/all_to_all | solution.py:330
  293.7 9.9 %all_to_all.120.sums_ref = f32[32,8,128]{2,1,0:T(8,128)S(1)} all-to-all(f32[32,8,128]{2,1,0:T(8,128)S(1)} %shard_map.115), channel_id=1, replica_groups=mesh['vox'=4,'fas'=8] {'vox','fas'}, dimensions={0} | all-to-all | bytes 262144 | tf_op jit(solution)/shard_map/all_to_all | solution.py:330
  303.6 1.9 shard_map.116
  305.5 16.2 %all_to_all.121.shares_ref = f32[8,96,128]{2,1,0:T(8,128)S(1)} all-to-all(f32[8,96,128]{2,1,0:T(8,128)S(1)} %bitcast.53), channel_id=1, replica_groups=mesh['vox'=4,'fas'=8] {'fas'}, dimensions={0} | all-to-all | bytes 786432 | tf_op jit(solution)/shard_map/all_to_all | solution.py:330
  321.7 15.3 %all_to_all.122 = f32[8,96,128]{2,1,0:T(8,128)S(1)} all-to-all(f32[8,96,128]{2,1,0:T(8,128)S(1)} %shard_map.117), channel_id=1, replica_groups=mesh['vox'=4,'fas'=8] {'fas'}, dimensions={0} | all-to-all | bytes 786432 | tf_op jit(solution)/shard_map/all_to_all | solution.py:330
  337.0 2.1 shard_map.118
  341.2 5.0 %collective-permute-done.9 = f32[256,128]{1,0:T(8,128)S(1)} collective-permute-done((f32[256,128]{1,0:T(8,128)S(1)}, f32[256,128]{1,0:T(8,128)S(1)}, u32[]{:S(2)}, u32[]{:S(2)}) %collective-permute-start.9) | collective-permute-done | bytes 131104 | tf_op jit(solution)/shard_map/ppermute | solution.py:355
  346.2 1.7 shard_map.119
  347.9 16.4 %all_to_all.123.shares_ref = f32[8,96,128]{2,1,0:T(8,128)S(1)} all-to-all(f32[8,96,128]{2,1,0:T(8,128)S(1)} %bitcast.59), channel_id=1, replica_groups=mesh['vox'=4,'fas'=8] {'fas'}, dimensions={0} | all-to-all | bytes 786432 | tf_op jit(solution)/shard_map/all_to_all | solution.py:330
  364.5 9.9 %all_to_all.124.sums_ref = f32[32,8,128]{2,1,0:T(8,128)S(1)} all-to-all(f32[32,8,128]{2,1,0:T(8,128)S(1)} %shard_map.120), channel_id=1, replica_groups=mesh['vox'=4,'fas'=8] {'vox','fas'}, dimensions={0} | all-to-all | bytes 262144 | tf_op jit(solution)/shard_map/all_to_all | solution.py:330
  374.4 1.7 shard_map.121
  376.5 1.4 reshape.117
  377.9 3.5 all-to-all-start.20
  382.1 12.4 %all-to-all-done.20 = f32[8,16,768]{2,1,0:T(8,128)S(1)} async-done(((f32[8,16,768]{2,1,0:T(8,128)}), f32[8,16,768]{2,1,0:T(8,128)S(1)}, u32[]{:S(2)}, u32[]{:S(2)}) %all-to-all-start.20) | async-done | bytes 393248 | tf_op jit(solution)/shard_map/all_to_all | solution.py:330
  (65 shorter events, 15.2 us)
Async XLA Ops:
  0.6 7.0 %copy-start.2 = (s32[256,64]{0,1:T(8,128)S(1)}, s32[256,64]{0,1:T(8,128)}, u32[]{:S(2)}) copy-start(s32[256,64]{0,1:T(8,128)} %param.13) | copy-start | bytes 196612
  0.6 7.2 %copy-start.3 = (f32[16,768]{1,0:T(8,128)S(1)}, f32[16,768]{1,0:T(8,128)}, u32[]{:S(2)}) copy-start(f32[16,768]{1,0:T(8,128)} %param.8) | copy-start | bytes 147460
  0.7 7.4 %copy-start.1 = (bf16[360,96]{0,1:T(8,128)(2,1)S(1)}, bf16[360,96]{0,1:T(8,128)(2,1)}, u32[]{:S(2)}) copy-start(bf16[360,96]{0,1:T(8,128)(2,1)} %param.15) | copy-start | bytes 207364
  7.6 4.7 %copy-start = (f32[32768]{0:T(1024)S(1)}, f32[32768]{0:T(1024)}, u32[]{:S(2)}) copy-start(f32[32768]{0:T(1024)} %param.9) | copy-start | bytes 393220
  54.9 1.4 collective-permute-start
  56.4 5.6 %collective-permute-start.1 = (f32[256,128]{1,0:T(8,128)S(1)}, f32[256,128]{1,0:T(8,128)S(1)}, u32[]{:S(2)}, u32[]{:S(2)}) collective-permute-start(f32[256,128]{1,0:T(8,128)S(1)} %add.78), channel_id=1, source_target_pairs={{0,16},{8,24},{16,0},{24,8},{1,17},{9,25},{17,1},{25,9},{2,18},{10... | collective-permute-start | bytes 393224 | tf_op jit(solution)/shard_map/ppermute | solution.py:355
  126.5 1.4 collective-permute-start.2
  128.0 5.6 %collective-permute-start.3 = (f32[256,128]{1,0:T(8,128)S(1)}, f32[256,128]{1,0:T(8,128)S(1)}, u32[]{:S(2)}, u32[]{:S(2)}) collective-permute-start(f32[256,128]{1,0:T(8,128)S(1)} %add.80), channel_id=1, source_target_pairs={{0,16},{8,24},{16,0},{24,8},{1,17},{9,25},{17,1},{25,9},{2,18},{10... | collective-permute-start | bytes 393224 | tf_op jit(solution)/shard_map/ppermute | solution.py:355
  197.5 1.4 collective-permute-start.4
  199.0 5.6 %collective-permute-start.5 = (f32[256,128]{1,0:T(8,128)S(1)}, f32[256,128]{1,0:T(8,128)S(1)}, u32[]{:S(2)}, u32[]{:S(2)}) collective-permute-start(f32[256,128]{1,0:T(8,128)S(1)} %add.82), channel_id=1, source_target_pairs={{0,16},{8,24},{16,0},{24,8},{1,17},{9,25},{17,1},{25,9},{2,18},{10... | collective-permute-start | bytes 393224 | tf_op jit(solution)/shard_map/ppermute | solution.py:355
  268.3 1.4 collective-permute-start.6
  269.7 5.6 %collective-permute-start.7 = (f32[256,128]{1,0:T(8,128)S(1)}, f32[256,128]{1,0:T(8,128)S(1)}, u32[]{:S(2)}, u32[]{:S(2)}) collective-permute-start(f32[256,128]{1,0:T(8,128)S(1)} %add.84), channel_id=1, source_target_pairs={{0,16},{8,24},{16,0},{24,8},{1,17},{9,25},{17,1},{25,9},{2,18},{10... | collective-permute-start | bytes 393224 | tf_op jit(solution)/shard_map/ppermute | solution.py:355
  339.1 1.4 collective-permute-start.8
  340.5 5.6 %collective-permute-start.9 = (f32[256,128]{1,0:T(8,128)S(1)}, f32[256,128]{1,0:T(8,128)S(1)}, u32[]{:S(2)}, u32[]{:S(2)}) collective-permute-start(f32[256,128]{1,0:T(8,128)S(1)} %add.86), channel_id=1, source_target_pairs={{0,16},{8,24},{16,0},{24,8},{1,17},{9,25},{17,1},{25,9},{2,18},{10... | collective-permute-start | bytes 393224 | tf_op jit(solution)/shard_map/ppermute | solution.py:355
  377.9 16.6 %all-to-all-start.20 = ((f32[8,16,768]{2,1,0:T(8,128)}), f32[8,16,768]{2,1,0:T(8,128)S(1)}, u32[]{:S(2)}, u32[]{:S(2)}) async-start(f32[8,16,768]{2,1,0:T(8,128)} %reshape.117), calls=%async_computation.20 | async-start | bytes 786432 | tf_op jit(solution)/shard_map/all_to_all | solution.py:330
where the time goes:
time: 395 us
  blocking collectives  297 us (75%)
  waiting for transfers between devices  43.1 us (11%)
  Pallas kernels  35.3 us (9%)
  starting transfers between devices  7.88 us (2%)
  local copies, waits for them, and re-layouts  4.86 us (1%)
  other arithmetic  4.46 us (1%)
    all_to_all x20, blocking collectives, swap(): return lax.all_to_all(x, axis, 0, 0)  297 us
    pallas_call x27, Pallas kernels, placed(): run(*(pltpu.with_memory_space_constraint(x, pltpu.VMEM) if kind == 'v' el...  35.3 us
    ppermute x10, waiting for transfers between devices, local(): lax.ppermute(gradient, 'vox', [(i, i ^ bit) for i in range(n_vox)])  30.7 us
    all_to_all x1, waiting for transfers between devices, swap(): return lax.all_to_all(x, axis, 0, 0)  12.4 us
  transfers between devices with their start and end apart: 11, of which 11 were waited for; matrix products, arithmetic and copies ran while one was open for 0% of the time, Pallas kernels for 0%

commit v1 on v0

--- a/solution.py
+++ b/solution.py
@@ -171,9 +171,9 @@
     acc_ref,
 ):
     sums = jnp.sum(sums_ref[...], axis=0)
-    upper = lax.broadcasted_iota(jnp.int32, (8, LANES), 0) < 4
-    image_sq = jnp.sum(jnp.where(upper, sums, 0.0), keepdims=True)
-    grad_sq = jnp.sum(jnp.where(upper, 0.0, sums), keepdims=True) * (1.0 / vox_total)
+    left = lane_ids(1) < BF
+    image_sq = jnp.sum(jnp.where(left, sums, 0.0), keepdims=True)
+    grad_sq = jnp.sum(jnp.where(left, 0.0, sums), keepdims=True) * (1.0 / vox_total)
     step = grad_sq / (image_sq + 1e-6)
     updated = jnp.maximum(w_ref[...] - step * p_ref[...], 0.0)
     new_ref[...] = updated
@@ -228,21 +228,23 @@
 
 
 def share_kernel(shares_ref, out_ref):
-    total = jnp.sum(shares_ref[...], axis=0)
+    out_ref[...] = jnp.sum(shares_ref[...], axis=0)
+
+
+def spread_kernel(mine_ref, other_ref, out_ref):
+    total = mine_ref[...] + other_ref[...]
     for i in range(out_ref.shape[0]):
         out_ref[i] = total
 
 
 def norm_kernel(shares_ref, sq_ref, out_ref):
     image = jnp.sum(shares_ref[...], axis=0)
-    image_sq = jnp.sum((image * image).reshape(-1, 8, LANES), axis=0)
-    sums = jnp.concatenate([image_sq[:4] + image_sq[4:], sq_ref[:4] + sq_ref[4:]], axis=0)
-
-    def copy_out(i, carry):
-        out_ref[i] = sums
-        return carry
-
-    lax.fori_loop(0, out_ref.shape[0], copy_out, 0)
+    image_sq = jnp.sum(image * image, axis=0, keepdims=True)
+    proj_sq = jnp.sum(sq_ref[...], axis=0, keepdims=True)
+    image_sq = image_sq + pltpu.roll(image_sq, BF, 1)
+    proj_sq = proj_sq + pltpu.roll(proj_sq, BF, 1)
+    sums = jnp.where(lane_ids(1) < BF, image_sq, proj_sq)
+    out_ref[...] = jnp.broadcast_to(sums[None], out_ref.shape)
 
 
 def call(kernel, outs, ins, scratch=()):
@@ -326,13 +328,21 @@
     image_out = ((image_rows, LANES), f32, "v")
     flat_out = ((half_rows, LANES), f32, "v")
 
-    def swap(x, axis):
-        return lax.all_to_all(x, axis, 0, 0)
-
+    def swap(x, axis, groups=None):
+        return lax.all_to_all(x, axis, 0, 0, axis_index_groups=groups)
+
+    half = n_fas // 2
+    halves = [list(range(half)), list(range(half, n_fas))]
+    across = [(i, (i + half) % n_fas) for i in range(n_fas)]
     share_rows = image_rows // n_fas
-
-    def collect(partial):
-        return swap(partial.reshape(n_fas, share_rows, LANES), "fas")
+    half_share = image_rows // half
+
+    def sum_all(partial):
+        shares = swap(partial.reshape(half, half_share, LANES), "fas", halves)
+        (mine,) = call(share_kernel, [((half_share, LANES), f32, "v")], "v")(shares)
+        other = lax.ppermute(mine, "fas", across)
+        (total,) = call(spread_kernel, [((half, half_share, LANES), f32, "v")], "vv")(mine, other)
+        return swap(total, "fas", halves).reshape(image_rows, LANES)
 
     weights = initial_weights.reshape(half_rows, LANES)
     (partial,) = call(
@@ -340,16 +350,13 @@
     )(meta, weights, sig, cp, a)
     for sweep in range(ITERS):
         last = sweep == ITERS - 1
-        (residual,) = call(share_kernel, [((n_fas, share_rows, LANES), f32, "v")], "v")(
-            collect(partial)
-        )
-        whole = swap(residual, "fas")
+        whole = sum_all(partial)
         (gradient,) = call(
             functools.partial(backward_kernel, cap, vox_rows),
             [flat_out],
             "svvv",
             [pltpu.VMEM((vox_rows, 2 * BV, LANES), bf16), table],
-        )(meta, whole.reshape(image_rows, LANES), cp, at)
+        )(meta, whole, cp, at)
         bit = 1
         while bit < n_vox:
             gradient = gradient + lax.ppermute(
@@ -362,9 +369,8 @@
             "svvvv",
             [table, acc],
         )(meta, gradient, weights, cp, a)
-        (sums,) = call(norm_kernel, [((n_vox * n_fas, 8, LANES), f32, "v")], "vv")(
-            collect(partial), proj_sq
-        )
+        shares = swap(partial.reshape(n_fas, share_rows, LANES), "fas")
+        (sums,) = call(norm_kernel, [((n_vox * n_fas, 1, LANES), f32, "v")], "vv")(shares, proj_sq)
         sums = swap(sums, ("vox", "fas"))
         out = ((vox_rows, BV, LANES), f32, "v") if last else image_out
         partial, weights = call(

time: 395 us -> 367 us (0.929)
  blocking collectives: 297 us -> 216 us
  waiting for transfers between devices: 43.1 us -> 71.3 us
  Pallas kernels: 35.3 us -> 53.6 us
  starting transfers between devices: 7.88 us -> 12.1 us
    all_to_all x20, blocking collectives: 297 us -> 216 us  [swap(): return lax.all_to_all(x, axis, 0, 0, axis_index_groups=groups)]
    ppermute x0 -> x5, waiting for transfers between devices: none -> 28.8 us  [sum_all(): other = lax.ppermute(mine, 'fas', across)]
    pallas_call x27 -> x32, Pallas kernels: 35.3 us -> 53.6 us  [placed(): run(*(pltpu.with_memory_space_constraint(x, pltpu.VMEM) if kind == 'v' el...]
    ppermute x0 -> x5, starting transfers between devices: none -> 4.79 us  [sum_all(): other = lax.ppermute(mine, 'fas', across)]
  transfers between devices with their start and end apart: 11 -> 16, of which waited for: 11 -> 16; matrix products, arithmetic and copies ran while one was open for 0% -> 0% of each run, Pallas kernels for 0% -> 0%
where the time goes in v1:
time: 367 us; the launch traced here: 365 us
  blocking collectives  216 us (59%)
  waiting for transfers between devices  71.3 us (19%)
  Pallas kernels  53.6 us (15%)
  starting transfers between devices  12.1 us (3%)
  local copies, waits for them, and re-layouts  4.85 us (1%)
  other arithmetic  4.46 us (1%)
    all_to_all x20, blocking collectives, swap(): return lax.all_to_all(x, axis, 0, 0, axis_index_groups=groups)  216 us
    pallas_call x32, Pallas kernels, placed(): run(*(pltpu.with_memory_space_constraint(x, pltpu.VMEM) if kind == 'v' el...  53.6 us
    ppermute x10, waiting for transfers between devices, local(): lax.ppermute(gradient, 'vox', [(i, i ^ bit) for i in range(n_vox)])  31.3 us
    ppermute x5, waiting for transfers between devices, sum_all(): other = lax.ppermute(mine, 'fas', across)  28.8 us
    all_to_all x1, waiting for transfers between devices, swap(): return lax.all_to_all(x, axis, 0, 0, axis_index_groups=groups)  11.2 us
  transfers between devices with their start and end apart: 16, of which 16 were waited for; matrix products, arithmetic and copies ran while one was open for 0% of the time, Pallas kernels for 0%

profile of v1, /device:TPU:0, one launch (start us, length us, event | category | flops | bytes accessed | tf_op | source)
XLA Modules:
  0.0 365.0 jit_solution(8927165081170763903)
XLA Ops:
  8.2 7.5 %shard_map.95 = (bf16[80,64,256]{2,1,0:T(8,128)(2,1)S(1)}, bf16[80,128,256]{2,1,0:T(8,128)(2,1)S(1)}, bf16[80,256,128]{2,1,0:T(8,128)(2,1)S(1)}) custom-call(s32[320]{0:T(512)S(1)} %broadcast_add_fusion.slot_ref, s32[1]{0:T(128)} %bitcast.1.turns_ref, bf16[256,32,128]{2,1,0:T(8,128)(2,1)S(1)} %bitcast.40, s32[256,128]{1,0:T(8,128)S(1)} %pad_add_fusion.atom_ref, ...), custom_call_target="tpu_custom_call" | custom-call | tf_op jit(solution)/shard_map/pallas_call | solution.py:265
  18.4 12.1 %all_to_all.105.shares_ref = f32[4,192,128]{2,1,0:T(8,128)S(1)} all-to-all(f32[4,192,128]{2,1,0:T(8,128)S(1)} %bitcast.46), channel_id=1, replica_groups={{0,1,2,3},{4,5,6,7},{8,9,10,11},{12,13,14,15},{16,17,18,19},{20,21,22,2..., dimensions={0} | all-to-all | bytes 786432 | tf_op jit(solution)/shard_map/all_to_all | solution.py:332
  32.5 5.1 %collective-permute-done.other_ref = f32[192,128]{1,0:T(8,128)S(1)} collective-permute-done((f32[192,128]{1,0:T(8,128)S(1)}, f32[192,128]{1,0:T(8,128)S(1)}, u32[]{:S(2)}, u32[]{:S(2)}) %collective-permute-start) | collective-permute-done | bytes 98336 | tf_op jit(solution)/shard_map/ppermute | solution.py:343
  37.6 9.6 %all_to_all.106 = f32[4,192,128]{2,1,0:T(8,128)S(1)} all-to-all(f32[4,192,128]{2,1,0:T(8,128)S(1)} %shard_map.98), channel_id=1, replica_groups={{0,1,2,3},{4,5,6,7},{8,9,10,11},{12,13,14,15},{16,17,18,19},{20,21,22,2..., dimensions={0} | all-to-all | bytes 786432 | tf_op jit(solution)/shard_map/all_to_all | solution.py:332
  47.2 3.1 shard_map.99
  52.3 5.0 %collective-permute-done.2 = f32[256,128]{1,0:T(8,128)S(1)} collective-permute-done((f32[256,128]{1,0:T(8,128)S(1)}, f32[256,128]{1,0:T(8,128)S(1)}, u32[]{:S(2)}, u32[]{:S(2)}) %collective-permute-start.2) | collective-permute-done | bytes 131104 | tf_op jit(solution)/shard_map/ppermute | solution.py:362
  57.4 2.6 shard_map.100
  60.0 14.2 %all_to_all.107.shares_ref = f32[8,96,128]{2,1,0:T(8,128)S(1)} all-to-all(f32[8,96,128]{2,1,0:T(8,128)S(1)} %bitcast.54), channel_id=1, replica_groups=mesh['vox'=4,'fas'=8] {'fas'}, dimensions={0} | all-to-all | bytes 786432 | tf_op jit(solution)/shard_map/all_to_all | solution.py:332
  74.4 10.0 %all_to_all.108.sums_ref = f32[32,1,128]{2,1,0:T(1,128)S(1)} all-to-all(f32[32,1,128]{2,1,0:T(1,128)S(1)} %shard_map.101), channel_id=1, replica_groups=mesh['vox'=4,'fas'=8] {'vox','fas'}, dimensions={0} | all-to-all | bytes 32768 | tf_op jit(solution)/shard_map/all_to_all | solution.py:332
  84.4 2.8 shard_map.102
  87.2 9.8 %all_to_all.109.shares_ref = f32[4,192,128]{2,1,0:T(8,128)S(1)} all-to-all(f32[4,192,128]{2,1,0:T(8,128)S(1)} %bitcast.55), channel_id=1, replica_groups={{0,1,2,3},{4,5,6,7},{8,9,10,11},{12,13,14,15},{16,17,18,19},{20,21,22,2..., dimensions={0} | all-to-all | bytes 786432 | tf_op jit(solution)/shard_map/all_to_all | solution.py:332
  97.7 5.9 %collective-permute-done.3.other_ref = f32[192,128]{1,0:T(8,128)S(1)} collective-permute-done((f32[192,128]{1,0:T(8,128)S(1)}, f32[192,128]{1,0:T(8,128)S(1)}, u32[]{:S(2)}, u32[]{:S(2)}) %collective-permute-start.3) | collective-permute-done | bytes 98336 | tf_op jit(solution)/shard_map/ppermute | solution.py:343
  103.7 8.8 %all_to_all.110 = f32[4,192,128]{2,1,0:T(8,128)S(1)} all-to-all(f32[4,192,128]{2,1,0:T(8,128)S(1)} %shard_map.104), channel_id=1, replica_groups={{0,1,2,3},{4,5,6,7},{8,9,10,11},{12,13,14,15},{16,17,18,19},{20,21,22,2..., dimensions={0} | all-to-all | bytes 786432 | tf_op jit(solution)/shard_map/all_to_all | solution.py:332
  112.5 3.1 shard_map.105
  117.8 4.9 %collective-permute-done.5 = f32[256,128]{1,0:T(8,128)S(1)} collective-permute-done((f32[256,128]{1,0:T(8,128)S(1)}, f32[256,128]{1,0:T(8,128)S(1)}, u32[]{:S(2)}, u32[]{:S(2)}) %collective-permute-start.5) | collective-permute-done | bytes 131104 | tf_op jit(solution)/shard_map/ppermute | solution.py:362
  122.7 2.6 shard_map.106
  125.3 14.2 %all_to_all.111.shares_ref = f32[8,96,128]{2,1,0:T(8,128)S(1)} all-to-all(f32[8,96,128]{2,1,0:T(8,128)S(1)} %bitcast.56), channel_id=1, replica_groups=mesh['vox'=4,'fas'=8] {'fas'}, dimensions={0} | all-to-all | bytes 786432 | tf_op jit(solution)/shard_map/all_to_all | solution.py:332
  139.7 9.7 %all_to_all.112.sums_ref = f32[32,1,128]{2,1,0:T(1,128)S(1)} all-to-all(f32[32,1,128]{2,1,0:T(1,128)S(1)} %shard_map.107), channel_id=1, replica_groups=mesh['vox'=4,'fas'=8] {'vox','fas'}, dimensions={0} | all-to-all | bytes 32768 | tf_op jit(solution)/shard_map/all_to_all | solution.py:332
  149.4 2.8 shard_map.108
  152.2 9.8 %all_to_all.113.shares_ref = f32[4,192,128]{2,1,0:T(8,128)S(1)} all-to-all(f32[4,192,128]{2,1,0:T(8,128)S(1)} %bitcast.51), channel_id=1, replica_groups={{0,1,2,3},{4,5,6,7},{8,9,10,11},{12,13,14,15},{16,17,18,19},{20,21,22,2..., dimensions={0} | all-to-all | bytes 786432 | tf_op jit(solution)/shard_map/all_to_all | solution.py:332
  162.7 5.9 %collective-permute-done.6.other_ref = f32[192,128]{1,0:T(8,128)S(1)} collective-permute-done((f32[192,128]{1,0:T(8,128)S(1)}, f32[192,128]{1,0:T(8,128)S(1)}, u32[]{:S(2)}, u32[]{:S(2)}) %collective-permute-start.6) | collective-permute-done | bytes 98336 | tf_op jit(solution)/shard_map/ppermute | solution.py:343
  168.7 8.8 %all_to_all.114 = f32[4,192,128]{2,1,0:T(8,128)S(1)} all-to-all(f32[4,192,128]{2,1,0:T(8,128)S(1)} %shard_map.110), channel_id=1, replica_groups={{0,1,2,3},{4,5,6,7},{8,9,10,11},{12,13,14,15},{16,17,18,19},{20,21,22,2..., dimensions={0} | all-to-all | bytes 786432 | tf_op jit(solution)/shard_map/all_to_all | solution.py:332
  177.5 3.3 shard_map.111
  183.0 4.9 %collective-permute-done.8 = f32[256,128]{1,0:T(8,128)S(1)} collective-permute-done((f32[256,128]{1,0:T(8,128)S(1)}, f32[256,128]{1,0:T(8,128)S(1)}, u32[]{:S(2)}, u32[]{:S(2)}) %collective-permute-start.8) | collective-permute-done | bytes 131104 | tf_op jit(solution)/shard_map/ppermute | solution.py:362
  187.9 2.6 shard_map.112
  190.5 14.2 %all_to_all.115.shares_ref = f32[8,96,128]{2,1,0:T(8,128)S(1)} all-to-all(f32[8,96,128]{2,1,0:T(8,128)S(1)} %bitcast.57), channel_id=1, replica_groups=mesh['vox'=4,'fas'=8] {'fas'}, dimensions={0} | all-to-all | bytes 786432 | tf_op jit(solution)/shard_map/all_to_all | solution.py:332
  204.8 9.7 %all_to_all.116.sums_ref = f32[32,1,128]{2,1,0:T(1,128)S(1)} all-to-all(f32[32,1,128]{2,1,0:T(1,128)S(1)} %shard_map.113), channel_id=1, replica_groups=mesh['vox'=4,'fas'=8] {'vox','fas'}, dimensions={0} | all-to-all | bytes 32768 | tf_op jit(solution)/shard_map/all_to_all | solution.py:332
  214.6 2.8 shard_map.114
  217.4 9.8 %all_to_all.117.shares_ref = f32[4,192,128]{2,1,0:T(8,128)S(1)} all-to-all(f32[4,192,128]{2,1,0:T(8,128)S(1)} %bitcast.52), channel_id=1, replica_groups={{0,1,2,3},{4,5,6,7},{8,9,10,11},{12,13,14,15},{16,17,18,19},{20,21,22,2..., dimensions={0} | all-to-all | bytes 786432 | tf_op jit(solution)/shard_map/all_to_all | solution.py:332
  227.9 5.9 %collective-permute-done.9.other_ref = f32[192,128]{1,0:T(8,128)S(1)} collective-permute-done((f32[192,128]{1,0:T(8,128)S(1)}, f32[192,128]{1,0:T(8,128)S(1)}, u32[]{:S(2)}, u32[]{:S(2)}) %collective-permute-start.9) | collective-permute-done | bytes 98336 | tf_op jit(solution)/shard_map/ppermute | solution.py:343
  233.9 8.8 %all_to_all.118 = f32[4,192,128]{2,1,0:T(8,128)S(1)} all-to-all(f32[4,192,128]{2,1,0:T(8,128)S(1)} %shard_map.116), channel_id=1, replica_groups={{0,1,2,3},{4,5,6,7},{8,9,10,11},{12,13,14,15},{16,17,18,19},{20,21,22,2..., dimensions={0} | all-to-all | bytes 786432 | tf_op jit(solution)/shard_map/all_to_all | solution.py:332
  242.7 3.1 shard_map.117
  248.0 4.9 %collective-permute-done.11 = f32[256,128]{1,0:T(8,128)S(1)} collective-permute-done((f32[256,128]{1,0:T(8,128)S(1)}, f32[256,128]{1,0:T(8,128)S(1)}, u32[]{:S(2)}, u32[]{:S(2)}) %collective-permute-start.11) | collective-permute-done | bytes 131104 | tf_op jit(solution)/shard_map/ppermute | solution.py:362
  252.9 2.6 shard_map.118
  255.5 14.2 %all_to_all.119.shares_ref = f32[8,96,128]{2,1,0:T(8,128)S(1)} all-to-all(f32[8,96,128]{2,1,0:T(8,128)S(1)} %bitcast.58), channel_id=1, replica_groups=mesh['vox'=4,'fas'=8] {'fas'}, dimensions={0} | all-to-all | bytes 786432 | tf_op jit(solution)/shard_map/all_to_all | solution.py:332
  269.9 9.7 %all_to_all.120.sums_ref = f32[32,1,128]{2,1,0:T(1,128)S(1)} all-to-all(f32[32,1,128]{2,1,0:T(1,128)S(1)} %shard_map.119), channel_id=1, replica_groups=mesh['vox'=4,'fas'=8] {'vox','fas'}, dimensions={0} | all-to-all | bytes 32768 | tf_op jit(solution)/shard_map/all_to_all | solution.py:332
  279.6 2.8 shard_map.120
  282.4 9.8 %all_to_all.121.shares_ref = f32[4,192,128]{2,1,0:T(8,128)S(1)} all-to-all(f32[4,192,128]{2,1,0:T(8,128)S(1)} %bitcast.53), channel_id=1, replica_groups={{0,1,2,3},{4,5,6,7},{8,9,10,11},{12,13,14,15},{16,17,18,19},{20,21,22,2..., dimensions={0} | all-to-all | bytes 786432 | tf_op jit(solution)/shard_map/all_to_all | solution.py:332
  292.9 5.9 %collective-permute-done.12.other_ref = f32[192,128]{1,0:T(8,128)S(1)} collective-permute-done((f32[192,128]{1,0:T(8,128)S(1)}, f32[192,128]{1,0:T(8,128)S(1)}, u32[]{:S(2)}, u32[]{:S(2)}) %collective-permute-start.12) | collective-permute-done | bytes 98336 | tf_op jit(solution)/shard_map/ppermute | solution.py:343
  298.8 8.8 %all_to_all.122 = f32[4,192,128]{2,1,0:T(8,128)S(1)} all-to-all(f32[4,192,128]{2,1,0:T(8,128)S(1)} %shard_map.122), channel_id=1, replica_groups={{0,1,2,3},{4,5,6,7},{8,9,10,11},{12,13,14,15},{16,17,18,19},{20,21,22,2..., dimensions={0} | all-to-all | bytes 786432 | tf_op jit(solution)/shard_map/all_to_all | solution.py:332
  307.7 3.1 shard_map.123
  313.0 4.9 %collective-permute-done.14 = f32[256,128]{1,0:T(8,128)S(1)} collective-permute-done((f32[256,128]{1,0:T(8,128)S(1)}, f32[256,128]{1,0:T(8,128)S(1)}, u32[]{:S(2)}, u32[]{:S(2)}) %collective-permute-start.14) | collective-permute-done | bytes 131104 | tf_op jit(solution)/shard_map/ppermute | solution.py:362
  317.9 2.6 shard_map.124
  320.5 14.2 %all_to_all.123.shares_ref = f32[8,96,128]{2,1,0:T(8,128)S(1)} all-to-all(f32[8,96,128]{2,1,0:T(8,128)S(1)} %bitcast.59), channel_id=1, replica_groups=mesh['vox'=4,'fas'=8] {'fas'}, dimensions={0} | all-to-all | bytes 786432 | tf_op jit(solution)/shard_map/all_to_all | solution.py:332
  334.9 9.7 %all_to_all.124.sums_ref = f32[32,1,128]{2,1,0:T(1,128)S(1)} all-to-all(f32[32,1,128]{2,1,0:T(1,128)S(1)} %shard_map.125), channel_id=1, replica_groups=mesh['vox'=4,'fas'=8] {'vox','fas'}, dimensions={0} | all-to-all | bytes 32768 | tf_op jit(solution)/shard_map/all_to_all | solution.py:332
  344.6 2.6 shard_map.126
  349.0 3.5 all-to-all-start.20
  353.1 11.2 %all-to-all-done.20 = f32[8,16,768]{2,1,0:T(8,128)S(1)} async-done(((f32[8,16,768]{2,1,0:T(8,128)}), f32[8,16,768]{2,1,0:T(8,128)S(1)}, u32[]{:S(2)}, u32[]{:S(2)}) %all-to-all-start.20) | async-done | bytes 393248 | tf_op jit(solution)/shard_map/all_to_all | solution.py:332
  (80 shorter events, 28.0 us)
Async XLA Ops:
  0.6 7.0 %copy-start.2 = (s32[256,64]{0,1:T(8,128)S(1)}, s32[256,64]{0,1:T(8,128)}, u32[]{:S(2)}) copy-start(s32[256,64]{0,1:T(8,128)} %param.13) | copy-start | bytes 196612
  0.6 7.2 %copy-start.3 = (f32[16,768]{1,0:T(8,128)S(1)}, f32[16,768]{1,0:T(8,128)}, u32[]{:S(2)}) copy-start(f32[16,768]{1,0:T(8,128)} %param.8) | copy-start | bytes 147460
  0.7 7.4 %copy-start.1 = (bf16[360,96]{0,1:T(8,128)(2,1)S(1)}, bf16[360,96]{0,1:T(8,128)(2,1)}, u32[]{:S(2)}) copy-start(bf16[360,96]{0,1:T(8,128)(2,1)} %param.15) | copy-start | bytes 207364
  7.6 8.1 %copy-start = (f32[32768]{0:T(1024)S(1)}, f32[32768]{0:T(1024)}, u32[]{:S(2)}) copy-start(f32[32768]{0:T(1024)} %param.9) | copy-start | bytes 393220
  30.5 7.1 %collective-permute-start = (f32[192,128]{1,0:T(8,128)S(1)}, f32[192,128]{1,0:T(8,128)S(1)}, u32[]{:S(2)}, u32[]{:S(2)}) collective-permute-start(f32[192,128]{1,0:T(8,128)S(1)} %shard_map.97.mine_ref), channel_id=1, source_target_pairs={{0,4},{1,5},{2,6},{3,7},{4,0},{5,1},{6,2},{7,3},{8,12},{9,13},{10,... | collective-permute-start | bytes 294920 | tf_op jit(solution)/shard_map/ppermute | solution.py:343
  50.3 1.4 collective-permute-start.1
  51.8 5.6 %collective-permute-start.2 = (f32[256,128]{1,0:T(8,128)S(1)}, f32[256,128]{1,0:T(8,128)S(1)}, u32[]{:S(2)}, u32[]{:S(2)}) collective-permute-start(f32[256,128]{1,0:T(8,128)S(1)} %add.78), channel_id=1, source_target_pairs={{0,16},{8,24},{16,0},{24,8},{1,17},{9,25},{17,1},{25,9},{2,18},{10... | collective-permute-start | bytes 393224 | tf_op jit(solution)/shard_map/ppermute | solution.py:362
  97.0 6.6 %collective-permute-start.3 = (f32[192,128]{1,0:T(8,128)S(1)}, f32[192,128]{1,0:T(8,128)S(1)}, u32[]{:S(2)}, u32[]{:S(2)}) collective-permute-start(f32[192,128]{1,0:T(8,128)S(1)} %shard_map.103.mine_ref), channel_id=1, source_target_pairs={{0,4},{1,5},{2,6},{3,7},{4,0},{5,1},{6,2},{7,3},{8,12},{9,13},{10,... | collective-permute-start | bytes 294920 | tf_op jit(solution)/shard_map/ppermute | solution.py:343
  115.6 1.4 collective-permute-start.4
  117.0 5.6 %collective-permute-start.5 = (f32[256,128]{1,0:T(8,128)S(1)}, f32[256,128]{1,0:T(8,128)S(1)}, u32[]{:S(2)}, u32[]{:S(2)}) collective-permute-start(f32[256,128]{1,0:T(8,128)S(1)} %add.80), channel_id=1, source_target_pairs={{0,16},{8,24},{16,0},{24,8},{1,17},{9,25},{17,1},{25,9},{2,18},{10... | collective-permute-start | bytes 393224 | tf_op jit(solution)/shard_map/ppermute | solution.py:362
  162.0 6.6 %collective-permute-start.6 = (f32[192,128]{1,0:T(8,128)S(1)}, f32[192,128]{1,0:T(8,128)S(1)}, u32[]{:S(2)}, u32[]{:S(2)}) collective-permute-start(f32[192,128]{1,0:T(8,128)S(1)} %shard_map.109.mine_ref), channel_id=1, source_target_pairs={{0,4},{1,5},{2,6},{3,7},{4,0},{5,1},{6,2},{7,3},{8,12},{9,13},{10,... | collective-permute-start | bytes 294920 | tf_op jit(solution)/shard_map/ppermute | solution.py:343
  180.8 1.4 collective-permute-start.7
  182.2 5.6 %collective-permute-start.8 = (f32[256,128]{1,0:T(8,128)S(1)}, f32[256,128]{1,0:T(8,128)S(1)}, u32[]{:S(2)}, u32[]{:S(2)}) collective-permute-start(f32[256,128]{1,0:T(8,128)S(1)} %add.82), channel_id=1, source_target_pairs={{0,16},{8,24},{16,0},{24,8},{1,17},{9,25},{17,1},{25,9},{2,18},{10... | collective-permute-start | bytes 393224 | tf_op jit(solution)/shard_map/ppermute | solution.py:362
  227.2 6.6 %collective-permute-start.9 = (f32[192,128]{1,0:T(8,128)S(1)}, f32[192,128]{1,0:T(8,128)S(1)}, u32[]{:S(2)}, u32[]{:S(2)}) collective-permute-start(f32[192,128]{1,0:T(8,128)S(1)} %shard_map.115.mine_ref), channel_id=1, source_target_pairs={{0,4},{1,5},{2,6},{3,7},{4,0},{5,1},{6,2},{7,3},{8,12},{9,13},{10,... | collective-permute-start | bytes 294920 | tf_op jit(solution)/shard_map/ppermute | solution.py:343
  245.8 1.4 collective-permute-start.10
  247.2 5.6 %collective-permute-start.11 = (f32[256,128]{1,0:T(8,128)S(1)}, f32[256,128]{1,0:T(8,128)S(1)}, u32[]{:S(2)}, u32[]{:S(2)}) collective-permute-start(f32[256,128]{1,0:T(8,128)S(1)} %add.84), channel_id=1, source_target_pairs={{0,16},{8,24},{16,0},{24,8},{1,17},{9,25},{17,1},{25,9},{2,18},{10... | collective-permute-start | bytes 393224 | tf_op jit(solution)/shard_map/ppermute | solution.py:362
  292.2 6.6 %collective-permute-start.12 = (f32[192,128]{1,0:T(8,128)S(1)}, f32[192,128]{1,0:T(8,128)S(1)}, u32[]{:S(2)}, u32[]{:S(2)}) collective-permute-start(f32[192,128]{1,0:T(8,128)S(1)} %shard_map.121.mine_ref), channel_id=1, source_target_pairs={{0,4},{1,5},{2,6},{3,7},{4,0},{5,1},{6,2},{7,3},{8,12},{9,13},{10,... | collective-permute-start | bytes 294920 | tf_op jit(solution)/shard_map/ppermute | solution.py:343
  310.8 1.4 collective-permute-start.13
  312.2 5.6 %collective-permute-start.14 = (f32[256,128]{1,0:T(8,128)S(1)}, f32[256,128]{1,0:T(8,128)S(1)}, u32[]{:S(2)}, u32[]{:S(2)}) collective-permute-start(f32[256,128]{1,0:T(8,128)S(1)} %add.86), channel_id=1, source_target_pairs={{0,16},{8,24},{16,0},{24,8},{1,17},{9,25},{17,1},{25,9},{2,18},{10... | collective-permute-start | bytes 393224 | tf_op jit(solution)/shard_map/ppermute | solution.py:362
  349.0 15.3 %all-to-all-start.20 = ((f32[8,16,768]{2,1,0:T(8,128)}), f32[8,16,768]{2,1,0:T(8,128)S(1)}, u32[]{:S(2)}, u32[]{:S(2)}) async-start(f32[8,16,768]{2,1,0:T(8,128)} %reshape.117), calls=%async_computation.20 | async-start | bytes 786432 | tf_op jit(solution)/shard_map/all_to_all | solution.py:332
